TPU v7x, 32 devices: a whole 2x2x4 slice. The times are simulated.
32 devices in a mesh: owner: 8 (over z, x), rep: 4 (over y, core).
Axes of the slice: x: 2, y: 2, z: 4, core: 2. Of those that a mesh axis runs over, the one named last changes fastest.
Arguments:
- stay_rows: bfloat16 [64, 256, 1024], P('owner', 'rep'), may hold values from -40 to 40
- stay_count: int32 [64, 4], P('owner', 'rep'), may hold values from 1 to 64, as said below
- moving_rows: bfloat16 [2048, 1024], P(('owner', 'rep')), may hold values from -5 to 5
- new_list: int32 [2048], P(('owner', 'rep')), may hold values from 0 to 63, as said below
- centroids: bfloat16 [64, 128, 1024], P('owner'), may hold values from -2 to 2
- sharpness: float32 [64], P('owner'), may hold values from 0.5 to 2
Outputs:
- refreshed: bfloat16 [64, 128, 1024], P('owner')
- mass: float32 [64, 128], P('owner', 'rep')
Inputs may be any that keep to these rules, and one draw needn't show every extreme that they name: `stay_count`: slots 0 to count - 1 of a list on a replica are live; some entry equals 64. `new_list`: within the rows of one device, each list is named at most 2 times, and on every device some list is named exactly 2 times.
All inputs are finite; a program needn't handle non-finite values.
Results may differ from a plain program's by a relative error of at most 0.0032.
Values may be sent and summed in bfloat16 or wider, within the bound.
A program may use at most 64 MiB of HBM per device.

v0:
```python
import math

import jax
import jax.numpy as jnp
from jax import lax
from jax.experimental import pallas as pl
from jax.experimental.pallas import tpu as pltpu
from jax.sharding import PartitionSpec as P

SLOT_L = 2


prior_weight = 1.0


def partner(value, axis, stride):
    mask = 2**stride
    pairs = [(source, source ^ mask) for source in range(lax.axis_size(axis))]
    return lax.ppermute(value, axis, pairs)


def weigh(members, live_mask, centres, centre_norm, sharp, features):
    products = jnp.einsum("lrd,lfd->lrf", members, centres, preferred_element_type=jnp.float32)
    scores = sharp[:, None, None] * (2.0 * products - centre_norm[:, None, :]) / math.sqrt(features)
    weights = jax.nn.softmax(scores, axis=-1).astype(jnp.bfloat16) * live_mask[:, :, None]
    numerator = jnp.einsum("lrf,lrd->lfd", weights, members, preferred_element_type=jnp.float32)
    return (numerator, jnp.sum(weights.astype(jnp.float32), axis=1))


def local(stay_rows, stay_count, moving_rows, new_list, centroids, sharpness):
    owners = lax.axis_size("owner")
    replicas = lax.axis_size("rep")
    lists_here, capacity, features = stay_rows.shape
    fine_count = centroids.shape[1]
    centre_norm = jnp.sum(jnp.square(centroids.astype(jnp.float32)), axis=-1)
    outgoing_count = new_list.shape[0]
    order_index = jnp.arange(outgoing_count)
    earlier = (new_list[None, :] == new_list[:, None]) & (
        order_index[None, :] < order_index[:, None]
    )
    slot_index = jnp.sum(earlier.astype(jnp.int32), axis=1)
    local_list = new_list % lists_here
    target_owner = new_list // lists_here
    position = (local_list * owners + target_owner) * SLOT_L + slot_index
    slot_total = lists_here * owners * SLOT_L
    outgoing = (
        jnp.zeros((slot_total, features), jnp.bfloat16)
        .at[position]
        .set(moving_rows, unique_indices=True)
    )
    occupied = (
        jnp.zeros((slot_total,), jnp.bfloat16)
        .at[position]
        .set(jnp.ones((outgoing_count,), jnp.bfloat16), unique_indices=True)
    )
    arrived, present = (
        lax.all_to_all(
            outgoing.reshape(lists_here, owners, SLOT_L, features),
            "owner",
            split_axis=1,
            concat_axis=1,
            tiled=True,
        ),
        lax.all_to_all(
            occupied.reshape(lists_here, owners, SLOT_L),
            "owner",
            split_axis=1,
            concat_axis=1,
            tiled=True,
        ),
    )
    arrive_slots = owners * SLOT_L
    arrivals = arrived.reshape(lists_here, arrive_slots, features)
    present = present.reshape(lists_here, arrive_slots)
    live_count = stay_count[:, 0]
    replica = lax.axis_index("rep")
    fine_share = fine_count // replicas
    groups = max(1, replicas // lists_here)
    per_rep = max(1, lists_here // replicas)
    slot_mask = (jnp.arange(capacity)[None, :] < live_count[:, None]).astype(jnp.bfloat16)
    stay_pieces = stay_rows.reshape(lists_here * groups, capacity // groups, features)
    mask_pieces = slot_mask.reshape(lists_here * groups, capacity // groups)
    moved_stay, moved_mask = (
        lax.all_to_all(stay_pieces, "rep", split_axis=0, concat_axis=1, tiled=True),
        lax.all_to_all(mask_pieces, "rep", split_axis=0, concat_axis=1, tiled=True),
    )
    arrive_pieces = arrivals.reshape(lists_here * groups, arrive_slots // groups, features)
    present_pieces = present.reshape(lists_here * groups, arrive_slots // groups)
    moved_arrive, moved_present = (
        lax.all_to_all(arrive_pieces, "rep", split_axis=0, concat_axis=1, tiled=True),
        lax.all_to_all(present_pieces, "rep", split_axis=0, concat_axis=1, tiled=True),
    )
    members = jnp.concatenate([moved_stay, moved_arrive], axis=1)
    member_mask = jnp.concatenate([moved_mask, moved_present], axis=1)
    first_list = replica * per_rep // groups
    centres = lax.dynamic_slice_in_dim(centroids, first_list, per_rep, 0)
    norms = lax.dynamic_slice_in_dim(centre_norm, first_list, per_rep, 0)
    sharp = lax.dynamic_slice_in_dim(sharpness, first_list, per_rep, 0)
    numerator, mass_sum = weigh(members, member_mask, centres, norms, sharp, features)
    for bit_number in range(groups.bit_length() - 1):
        other_num, other_mass = partner((numerator, mass_sum), "rep", bit_number)
        numerator = numerator + other_num
        mass_sum = mass_sum + other_mass
    refreshed_all = (
        (numerator + prior_weight * centres.astype(jnp.float32))
        / (mass_sum[:, :, None] + prior_weight)
    ).astype(jnp.bfloat16)
    piece_rows = fine_count // groups
    part_index = replica % groups
    refreshed_piece = lax.dynamic_slice_in_dim(
        refreshed_all, part_index * piece_rows, piece_rows, 1
    ).reshape(per_rep * piece_rows, features)
    mass_piece = lax.dynamic_slice_in_dim(mass_sum, part_index * piece_rows, piece_rows, 1).reshape(
        per_rep * piece_rows
    )
    refreshed = lax.all_gather(refreshed_piece, "rep", axis=0, tiled=True).reshape(
        lists_here, fine_count, features
    )
    mass_whole = lax.all_gather(mass_piece, "rep", axis=0, tiled=True).reshape(
        lists_here, fine_count
    )
    return (refreshed, lax.dynamic_slice_in_dim(mass_whole, replica * fine_share, fine_share, 1))


LANES = 128
VMEM_BUDGET = 40 * 2**20
MESH = pl.DeviceIdType.MESH


class Plan:
    def __init__(self, owners, replicas, lists, capacity, features, fine, moving):
        self.owners, self.replicas, self.lists = owners, replicas, lists
        self.capacity, self.features, self.fine, self.moving = capacity, features, fine, moving
        self.split = 2 if replicas % 2 == 0 and lists % 2 == 0 else 1
        self.groups = replicas // self.split
        self.half = lists // self.split
        self.per_source = self.half * SLOT_L
        self.block = self.groups * self.per_source
        self.blocks = owners * self.split
        self.width = features + LANES
        self.moving_lanes = -(-moving // LANES) * LANES

    def fits(self):
        slots = 2 * self.blocks * self.block * self.width
        held = self.half * self.replicas * self.capacity * self.features
        centres = 2 * self.half * self.fine * self.features
        gathered = self.groups * self.moving * self.features
        small = 2 * (slots + held + centres + gathered)
        return (
            small <= VMEM_BUDGET
            and self.block % 16 == 0
            and self.capacity % 16 == 0
            and self.moving % 16 == 0
            and self.features % LANES == 0
            and self.fine % LANES == 0
        )


def weigh_rows(plan, centres, norm, sharp, rows, mask):
    products = lax.dot_general(
        centres, rows, (((1,), (1,)), ((), ())), preferred_element_type=jnp.float32
    )
    scores = sharp * (2.0 * products - norm) / math.sqrt(plan.features)
    top = jnp.max(scores, axis=0, keepdims=True)
    raised = jnp.exp(scores - top)
    weights = (raised / jnp.sum(raised, axis=0, keepdims=True)).astype(jnp.bfloat16)
    weights = weights * mask.astype(jnp.bfloat16)
    numerator = jnp.dot(weights, rows, preferred_element_type=jnp.float32)
    mass = jnp.sum(weights.astype(jnp.float32), axis=1, keepdims=True)
    ones = jnp.ones((8, rows.shape[0]), jnp.bfloat16)
    mass_row = lax.dot_general(
        ones, weights, (((1,), (1,)), ((), ())), preferred_element_type=jnp.float32
    )
    return numerator, mass, mass_row


def fused_kernel(
    plan,
    stay_ref, count_in, moving_ref, list_in, centre_ref, sharp_in,
    out_ref, mass_ref,
    count_ref, moving_own, list_ref, sharp_ref, operand_sem, total_buf, mass_col,
    stay_buf, count_buf, moving_buf, pos_own, pos_buf, placed, arrived, centre_buf, result_buf, mass_buf,
    stay_send, stay_recv, count_send, count_recv, moving_send, moving_recv, pos_send, pos_recv,
    slot_send, slot_recv, centre_sem, result_send, result_recv, mass_send, mass_recv, local_sem,
):
    owners, split, groups, half = plan.owners, plan.split, plan.groups, plan.half
    replicas, capacity, features = plan.replicas, plan.capacity, plan.features
    owner = lax.axis_index("owner")
    replica = lax.axis_index("rep")
    core = replica % split
    group = replica // split

    def rep_at(k, dc):
        return lax.rem(group + k, groups) * split + lax.rem(core + dc, split)

    def owner_at(k):
        return lax.rem(owner + k, owners)

    peers = [(k, dc) for k in range(groups) for dc in range(split) if (k, dc) != (0, 0)]
    plane = [(k, dc) for k in range(1, owners) for dc in range(split)]
    barrier = pltpu.get_barrier_semaphore()
    for k, dc in peers:
        pl.semaphore_signal(barrier, inc=1, device_id=(owner, rep_at(k, dc)), device_id_type=MESH)
    for k, dc in plane:
        pl.semaphore_signal(
            barrier, inc=1, device_id=(owner_at(k), rep_at(0, dc)), device_id_type=MESH
        )

    small = [
        pltpu.make_async_copy(source, held, operand_sem.at[i])
        for i, (source, held) in enumerate([
            (list_in, list_ref), (count_in, count_ref), (moving_ref, moving_own), (sharp_in, sharp_ref),
        ])
    ]
    for copy in small:
        copy.start()
    centre_copy = pltpu.make_async_copy(
        centre_ref.at[pl.ds(core * half, half)], centre_buf, centre_sem
    )
    centre_copy.start()

    def own_copy(j):
        return pltpu.make_async_copy(
            stay_ref.at[core * half + j], stay_buf.at[j, 0], stay_recv.at[j, 0]
        )

    for j in range(half):
        own_copy(j).start()

    moving = plan.moving
    small[0].wait()
    small[1].wait()
    line = lax.broadcasted_iota(jnp.int32, count_buf.shape[1:], 0)
    live = jnp.zeros(count_buf.shape[1:], jnp.int32)
    for i in range(plan.lists):
        live = jnp.where(line == i, count_ref[i], live)
    count_buf[0] = live
    names = jnp.broadcast_to(list_ref[...], (moving, moving))
    row = lax.broadcasted_iota(jnp.int32, (moving, moving), 0)
    column = lax.broadcasted_iota(jnp.int32, (moving, moving), 1)
    down = jnp.sum(jnp.where(row == column, names, 0), axis=1, keepdims=True)
    earlier = jnp.where((names == down) & (row < column), 1, 0)
    slot = jnp.sum(earlier, axis=0, keepdims=True)
    target = list_ref[...]
    position = (
        (target // half) * plan.block + group * plan.per_source + (target % half) * SLOT_L + slot
    )
    pos_own[...] = jnp.full(pos_own.shape, -1, jnp.int32)
    pos_own[:, :moving] = jnp.broadcast_to(position, (8, moving))

    pl.semaphore_wait(barrier, len(peers) + len(plane))

    def moving_copy(k):
        return pltpu.make_async_remote_copy(
            src_ref=moving_ref, dst_ref=moving_buf.at[k - 1],
            send_sem=moving_send.at[k - 1], recv_sem=moving_recv.at[k - 1],
            device_id=(owner, rep_at(k, 0)), device_id_type=MESH,
        )

    def pos_copy(k):
        return pltpu.make_async_remote_copy(
            src_ref=pos_own, dst_ref=pos_buf.at[k - 1],
            send_sem=pos_send.at[k - 1], recv_sem=pos_recv.at[k - 1],
            device_id=(owner, rep_at(k, 0)), device_id_type=MESH,
        )

    for k in range(1, groups):
        pos_copy(k).start()
        moving_copy(k).start()

    def count_copy(k, dc):
        q = k * split + dc
        return pltpu.make_async_remote_copy(
            src_ref=count_buf.at[0], dst_ref=count_buf.at[q],
            send_sem=count_send.at[q], recv_sem=count_recv.at[q],
            device_id=(owner, rep_at(k, dc)), device_id_type=MESH,
        )

    def stay_copy(j, k, dc):
        q = k * split + dc
        return pltpu.make_async_remote_copy(
            src_ref=stay_ref.at[lax.rem(core + dc, split) * half + j], dst_ref=stay_buf.at[j, q],
            send_sem=stay_send.at[j, q], recv_sem=stay_recv.at[j, q],
            device_id=(owner, rep_at(k, dc)), device_id_type=MESH,
        )

    for k, dc in peers:
        count_copy(k, dc).start()
    ahead = min(2, half)
    small[2].wait()
    small[3].wait()

    total = plan.blocks * plan.block
    slot_row = lax.broadcasted_iota(jnp.int32, (total, moving), 0)

    def one_hot(positions):
        return jnp.where(slot_row == positions, 1.0, 0.0).astype(jnp.bfloat16)

    pick = one_hot(pos_own[0:1, :moving])
    ones = jnp.ones((moving, LANES), jnp.bfloat16)
    rows = jnp.dot(pick, moving_own[...], preferred_element_type=jnp.float32)
    flags = jnp.dot(pick, ones, preferred_element_type=jnp.float32)
    for k in range(1, groups):
        pos_copy(k).wait_send()
        moving_copy(k).wait_send()
    for j in range(ahead):
        for k, dc in peers:
            stay_copy(j, k, dc).start()
    for k in range(1, groups):
        pos_copy(k).wait_recv()
        moving_copy(k).wait_recv()
        pick = one_hot(pos_buf[k - 1, 0:1, :moving])
        rows += jnp.dot(pick, moving_buf[k - 1], preferred_element_type=jnp.float32)
        flags += jnp.dot(pick, ones, preferred_element_type=jnp.float32)
    placed[:, :, :features] = rows.astype(jnp.bfloat16).reshape(plan.blocks, plan.block, features)
    placed[:, :, features:] = flags.astype(jnp.bfloat16).reshape(plan.blocks, plan.block, LANES)

    def slot_copy(k, dc):
        b = k * split + dc
        return pltpu.make_async_remote_copy(
            src_ref=placed.at[owner_at(k) * split + lax.rem(core + dc, split)],
            dst_ref=arrived.at[b],
            send_sem=slot_send.at[b], recv_sem=slot_recv.at[b],
            device_id=(owner_at(k), rep_at(0, dc)), device_id_type=MESH,
        )

    sent = [(k, dc) for k in range(owners) for dc in range(split) if (k, dc) != (0, 0)]
    for k, dc in sent:
        slot_copy(k, dc).start()
    arrived[0] = placed[owner * split + core]
    centre_copy.wait()
    for k, dc in peers:
        count_copy(k, dc).wait_recv()

    arrived_lane = lax.broadcasted_iota(jnp.int32, (1, total), 1)
    arrived_list = (arrived_lane % plan.per_source) // SLOT_L

    def result_copy(j, dc):
        return pltpu.make_async_remote_copy(
            src_ref=result_buf.at[j], dst_ref=out_ref.at[core * half + j],
            send_sem=result_send.at[j, dc], recv_sem=result_recv.at[j, dc],
            device_id=(owner, rep_at(0, dc)), device_id_type=MESH,
        )

    def result_own(j):
        return pltpu.make_async_copy(
            result_buf.at[j], out_ref.at[core * half + j], result_recv.at[j, 0]
        )

    def list_facts(j):
        centres = centre_buf[j]
        wide = centres.astype(jnp.float32)
        norm = jnp.sum(wide * wide, axis=1, keepdims=True)
        return centres, norm, sharp_ref[core * half + j]

    def add_part(j, rows, mask):
        num, mass, mass_row = weigh_rows(plan, *list_facts(j), rows, mask)
        total_buf[j] += num
        mass_col[j] += jnp.broadcast_to(mass, mass_col.shape[1:])
        mass_buf[j] += mass_row

    def add_stay(j, first, last):
        lane = lax.broadcasted_iota(jnp.int32, (1, (last - first) * capacity), 1)
        counts = jnp.zeros(lane.shape, jnp.int32)
        for q in range(first, last):
            counts = jnp.where(
                lane // capacity == q - first,
                count_buf[q, pl.ds(core * half + j, 1), :][:, : lane.shape[1]], counts,
            )
        mask = jnp.where(lane % capacity < counts, 1.0, 0.0)
        members = stay_buf[j, first:last].reshape((last - first) * capacity, features)
        add_part(j, members, mask)

    def add_arrivals(j):
        spread = jnp.full((8, LANES), 1.0 / LANES, jnp.bfloat16)
        marks = arrived[:, :, features:].reshape(total, LANES)
        present = lax.dot_general(
            spread, marks, (((1,), (1,)), ((), ())), preferred_element_type=jnp.float32
        )[0:1]
        here = jnp.where(arrived_list == j, present, 0.0)
        add_part(j, arrived[:, :, :features].reshape(total, features), here)

    def add_near(j):
        total_buf[j] = prior_weight * centre_buf[j].astype(jnp.float32)
        mass_col[j] = jnp.zeros(mass_col.shape[1:], jnp.float32)
        mass_buf[j] = jnp.zeros(mass_buf.shape[1:], jnp.float32)
        own_copy(j).wait()
        for k, dc in peers:
            if k == 0:
                stay_copy(j, k, dc).wait_recv()
        add_stay(j, 0, split)

    def pass_on(j):
        for k, dc in peers:
            stay_copy(j, k, dc).wait_send()

        @pl.when(j + ahead < half)
        def _():
            for k, dc in peers:
                stay_copy(j + ahead, k, dc).start()

    def add_far(j):
        for k, dc in peers:
            if k > 0:
                stay_copy(j, k, dc).wait_recv()
        if groups > 1:
            add_stay(j, split, replicas)

    def finish(j):
        share = 1.0 / (mass_col[j][:, 0:1] + prior_weight)
        result_buf[j] = (total_buf[j] * share).astype(jnp.bfloat16)
        result_own(j).start()
        for dc in range(1, split):
            result_copy(j, dc).start()

    def early(j, carry):
        add_near(j)
        pass_on(j)
        add_far(j)
        return carry

    def settle(j, carry):
        add_arrivals(j)
        finish(j)
        return carry

    def late(j, carry):
        add_near(j)
        add_arrivals(j)
        pass_on(j)
        add_far(j)
        finish(j)
        return carry

    cut = half - ahead
    lax.fori_loop(0, cut, early, 0)
    for k, dc in sent:
        slot_copy(k, dc).wait_recv()
    lax.fori_loop(0, cut, settle, 0)
    lax.fori_loop(cut, half, late, 0)

    def mass_copy(dc):
        return pltpu.make_async_remote_copy(
            src_ref=mass_buf, dst_ref=mass_ref.at[core],
            send_sem=mass_send.at[dc], recv_sem=mass_recv.at[dc],
            device_id=(owner, rep_at(0, dc)), device_id_type=MESH,
        )

    mass_own = pltpu.make_async_copy(mass_buf, mass_ref.at[core], local_sem)
    mass_own.start()
    for dc in range(1, split):
        mass_copy(dc).start()

    for k, dc in peers:
        count_copy(k, dc).wait_send()
    for k, dc in sent:
        slot_copy(k, dc).wait_send()
    for j in range(half):
        result_own(j).wait()
        for dc in range(1, split):
            result_copy(j, dc).wait()
    mass_own.wait()
    for dc in range(1, split):
        mass_copy(dc).wait()


def fused(plan, stay_rows, stay_count, moving_rows, new_list, centroids, sharpness):
    half, split, replicas = plan.half, plan.split, plan.replicas
    any_space = pl.BlockSpec(memory_space=pl.ANY)
    dma = pltpu.SemaphoreType.DMA
    members = replicas * plan.capacity
    refreshed, mass = pl.pallas_call(
        lambda *refs: fused_kernel(plan, *refs),
        out_shape=(
            jax.ShapeDtypeStruct(centroids.shape, jnp.bfloat16),
            jax.ShapeDtypeStruct((split, half, 8, plan.fine), jnp.float32),
        ),
        in_specs=[pl.BlockSpec(memory_space=pltpu.HBM)] * 6,
        out_specs=(any_space, any_space),
        scratch_shapes=[
            pltpu.SMEM((plan.lists,), jnp.int32),
            pltpu.VMEM((plan.moving, plan.features), jnp.bfloat16),
            pltpu.VMEM((1, plan.moving), jnp.int32),
            pltpu.SMEM((plan.lists,), jnp.float32),
            dma((4,)),
            pltpu.VMEM((half, plan.fine, plan.features), jnp.float32),
            pltpu.VMEM((half, plan.fine, LANES), jnp.float32),
            pltpu.VMEM((half, replicas, plan.capacity, plan.features), jnp.bfloat16),
            pltpu.VMEM((replicas, plan.lists, members), jnp.int32),
            pltpu.VMEM((max(1, plan.groups - 1), plan.moving, plan.features), jnp.bfloat16),
            pltpu.VMEM((8, plan.moving_lanes), jnp.int32),
            pltpu.VMEM((max(1, plan.groups - 1), 8, plan.moving_lanes), jnp.int32),
            pltpu.VMEM((plan.blocks, plan.block, plan.width), jnp.bfloat16),
            pltpu.VMEM((plan.blocks, plan.block, plan.width), jnp.bfloat16),
            pltpu.VMEM((half, plan.fine, plan.features), jnp.bfloat16),
            pltpu.VMEM((half, plan.fine, plan.features), jnp.bfloat16),
            pltpu.VMEM((half, 8, plan.fine), jnp.float32),
            dma((half, replicas)), dma((half, replicas)),
            dma((replicas,)), dma((replicas,)),
            dma((plan.groups,)), dma((plan.groups,)),
            dma((plan.groups,)), dma((plan.groups,)),
            dma((plan.blocks,)), dma((plan.blocks,)),
            dma,
            dma((half, split)), dma((half, split)),
            dma((split,)), dma((split,)),
            dma,
        ],
        compiler_params=pltpu.CompilerParams(
            collective_id=0, has_side_effects=True, vmem_limit_bytes=58500 * 2**10
        ),
    )(stay_rows, stay_count.reshape(-1), moving_rows, new_list.reshape(1, -1), centroids, sharpness)
    fine_share = plan.fine // replicas
    whole = mass[:, :, 0, :].reshape(plan.lists, plan.fine)
    share = lax.dynamic_slice_in_dim(whole, lax.axis_index("rep") * fine_share, fine_share, 1)
    return refreshed, share


def device_program(stay_rows, stay_count, moving_rows, new_list, centroids, sharpness):
    lists_here, capacity, features = stay_rows.shape
    plan = Plan(
        lax.axis_size("owner"), lax.axis_size("rep"), lists_here, capacity, features,
        centroids.shape[1], moving_rows.shape[0],
    )
    step = (lambda *a: fused(plan, *a)) if plan.fits() else local
    return step(stay_rows, stay_count, moving_rows, new_list, centroids, sharpness)


def solution(mesh):
    in_specs = (
        P("owner", "rep", None),
        P("owner", "rep"),
        P(("owner", "rep"), None),
        P(("owner", "rep")),
        P("owner", None, None),
        P("owner"),
    )
    out_specs = (P("owner", None, None), P("owner", "rep"))
    return jax.shard_map(device_program, mesh=mesh, in_specs=in_specs, out_specs=out_specs, check_vma=False)
```

profile of v0, /device:TPU:0, one launch (start us, length us, event | category | flops | bytes accessed | tf_op | source)
XLA Modules:
  0.0 42.2 jit_solution(5694744515761979190)
XLA Ops:
  0.6 37.0 %shard_map.77 = (bf16[8,128,1024]{2,1,0:T(8,128)(2,1)}, f32[2,4,8,128]{3,2,1,0:T(8,128)}) custom-call(bf16[8,64,1024]{2,1,0:T(8,128)(2,1)} %refs_0_.1, s32[8]{0:T(128)} %bitcast.4, bf16[64,1024]{1,0:T(8,128)(2,1)} %refs_2_.1, s32[1,64]{1,0:T(1,128)} %bitcast.5, bf16[8,128,1024]{2,1,0:T(8,128)(2,1)} %refs_4_.1, f32[8]{0:T(128)} %refs_5_.1), custom_call_target="tpu_custom_call" | custom-call | tf_op jit(solution)/shard_map/pallas_call | solution.py:472
  37.7 0.8 %slice.3 = f32[2,4,1,128]{3,2,1,0:T(1,128)S(1)} slice(f32[2,4,8,128]{3,2,1,0:T(8,128)} %get-tuple-element.5), slice={[0:2], [0:4], [0:1], [0:128]} | slice | bytes 8192 | tf_op jit(solution)/shard_map/slice | solution.py:513
  38.4 0.7 %constant_dynamic-slice_fusion = f32[8,32]{1,0:T(8,128)} fusion(f32[8,128]{1,0:T(8,128)S(1)} %bitcast.3, s32[]{:T(128)S(6)} %select_n.3), kind=kLoop, calls=%fused_computation | loop fusion | bytes 2052 | tf_op jit(solution)/shard_map/dynamic_slice | solution.py:514
  39.1 3.1 %copy.9 = bf16[8,128,1024]{2,1,0:T(8,128)(2,1)} copy(bf16[8,128,1024]{2,1,0:T(8,128)(2,1)} %get-tuple-element.8) | data formatting | bytes 4194304
where the time goes:
time: 42.4 us; the launch traced here: 42.2 us
  Pallas kernels  37 us (87%)
  local copies, waits for them, and re-layouts  4.51 us (11%)
  between operations  0.64 us (2%)
    pallas_call x1, Pallas kernels, fused(): pl.pallas_call(lambda *refs: fused_kernel(plan, *refs), out_shape=(jax.Sh...  37 us
    unnamed x1, local copies, waits for them, and re-layouts  3.08 us

commit v1 on v0

--- a/solution.py
+++ b/solution.py
@@ -124,6 +124,7 @@
 
 LANES = 128
 VMEM_BUDGET = 40 * 2**20
+VMEM_GRANT = 60000 * 2**10
 MESH = pl.DeviceIdType.MESH
 
 
@@ -286,7 +287,11 @@
 
     for k, dc in peers:
         count_copy(k, dc).start()
-    ahead = min(2, half)
+    siblings = [(k, dc) for k, dc in peers if k == 0]
+    distant = [(k, dc) for k, dc in peers if k > 0]
+    for j in range(half):
+        for k, dc in siblings:
+            stay_copy(j, k, dc).start()
     small[2].wait()
     small[3].wait()
 
@@ -303,9 +308,8 @@
     for k in range(1, groups):
         pos_copy(k).wait_send()
         moving_copy(k).wait_send()
-    for j in range(ahead):
-        for k, dc in peers:
-            stay_copy(j, k, dc).start()
+    for k, dc in distant:
+        stay_copy(0, k, dc).start()
     for k in range(1, groups):
         pos_copy(k).wait_recv()
         moving_copy(k).wait_recv()
@@ -385,24 +389,18 @@
         mass_col[j] = jnp.zeros(mass_col.shape[1:], jnp.float32)
         mass_buf[j] = jnp.zeros(mass_buf.shape[1:], jnp.float32)
         own_copy(j).wait()
-        for k, dc in peers:
-            if k == 0:
-                stay_copy(j, k, dc).wait_recv()
+        for k, dc in siblings:
+            stay_copy(j, k, dc).wait_recv()
         add_stay(j, 0, split)
 
     def pass_on(j):
-        for k, dc in peers:
+        for k, dc in distant:
             stay_copy(j, k, dc).wait_send()
-
-        @pl.when(j + ahead < half)
-        def _():
-            for k, dc in peers:
-                stay_copy(j + ahead, k, dc).start()
+            stay_copy(j + 1, k, dc).start()
 
     def add_far(j):
-        for k, dc in peers:
-            if k > 0:
-                stay_copy(j, k, dc).wait_recv()
+        for k, dc in distant:
+            stay_copy(j, k, dc).wait_recv()
         if groups > 1:
             add_stay(j, split, replicas)
 
@@ -424,20 +422,15 @@
         finish(j)
         return carry
 
-    def late(j, carry):
-        add_near(j)
-        add_arrivals(j)
-        pass_on(j)
-        add_far(j)
-        finish(j)
-        return carry
-
-    cut = half - ahead
-    lax.fori_loop(0, cut, early, 0)
+    last = half - 1
+    lax.fori_loop(0, last, early, 0)
+    add_near(last)
     for k, dc in sent:
         slot_copy(k, dc).wait_recv()
-    lax.fori_loop(0, cut, settle, 0)
-    lax.fori_loop(cut, half, late, 0)
+    lax.fori_loop(0, last, settle, 0)
+    add_arrivals(last)
+    add_far(last)
+    finish(last)
 
     def mass_copy(dc):
         return pltpu.make_async_remote_copy(
@@ -453,6 +446,11 @@
 
     for k, dc in peers:
         count_copy(k, dc).wait_send()
+    for k, dc in distant:
+        stay_copy(last, k, dc).wait_send()
+    for j in range(half):
+        for k, dc in siblings:
+            stay_copy(j, k, dc).wait_send()
     for k, dc in sent:
         slot_copy(k, dc).wait_send()
     for j in range(half):
@@ -462,6 +460,24 @@
     mass_own.wait()
     for dc in range(1, split):
         mass_copy(dc).wait()
+
+
+def deliver_kernel(plan, made_ref, mass_ref, out_ref, share_ref, sems):
+    copies = [
+        pltpu.make_async_copy(made_ref.at[i], out_ref.at[i], sems.at[i]) for i in range(plan.lists)
+    ]
+    for copy in copies:
+        copy.start()
+    replica = lax.axis_index("rep")
+    width = plan.fine // plan.replicas
+    rows = [mass_ref[s, j, 0:1, :] for s in range(plan.split) for j in range(plan.half)]
+    whole = jnp.concatenate(rows, axis=0)
+    share = whole[:, :width]
+    for r in range(1, plan.replicas):
+        share = jnp.where(replica == r, whole[:, r * width : (r + 1) * width], share)
+    share_ref[...] = share
+    for copy in copies:
+        copy.wait()
 
 
 def fused(plan, stay_rows, stay_count, moving_rows, new_list, centroids, sharpness):
@@ -506,13 +522,20 @@
             dma,
         ],
         compiler_params=pltpu.CompilerParams(
-            collective_id=0, has_side_effects=True, vmem_limit_bytes=58500 * 2**10
+            collective_id=0, has_side_effects=True, vmem_limit_bytes=VMEM_GRANT
         ),
     )(stay_rows, stay_count.reshape(-1), moving_rows, new_list.reshape(1, -1), centroids, sharpness)
-    fine_share = plan.fine // replicas
-    whole = mass[:, :, 0, :].reshape(plan.lists, plan.fine)
-    share = lax.dynamic_slice_in_dim(whole, lax.axis_index("rep") * fine_share, fine_share, 1)
-    return refreshed, share
+    return pl.pallas_call(
+        lambda *refs: deliver_kernel(plan, *refs),
+        out_shape=(
+            jax.ShapeDtypeStruct(centroids.shape, jnp.bfloat16),
+            jax.ShapeDtypeStruct((plan.lists, plan.fine // replicas), jnp.float32),
+        ),
+        in_specs=[any_space, pl.BlockSpec(memory_space=pltpu.VMEM)],
+        out_specs=(any_space, pl.BlockSpec(memory_space=pltpu.VMEM)),
+        scratch_shapes=[dma((plan.lists,))],
+        compiler_params=pltpu.CompilerParams(vmem_limit_bytes=VMEM_GRANT),
+    )(refreshed, mass)
 
 
 def device_program(stay_rows, stay_count, moving_rows, new_list, centroids, sharpness):

time: 42.4 us -> 104 us (2.45)
  Pallas kernels: 37 us -> 103 us
  local copies, waits for them, and re-layouts: 4.51 us -> 0 us
    pallas_call x0 -> x1, Pallas kernels: none -> 66 us  [fused(): pl.pallas_call(lambda *refs: deliver_kernel(plan, *refs), out_shape=(jax....]
    unnamed x1 -> x0, local copies, waits for them, and re-layouts: 3.08 us -> none
where the time goes in v1:
time: 104 us
  Pallas kernels  103 us (99%)
    pallas_call x1, Pallas kernels, fused(): pl.pallas_call(lambda *refs: deliver_kernel(plan, *refs), out_shape=(jax....  66 us
    pallas_call x1, Pallas kernels, fused(): pl.pallas_call(lambda *refs: fused_kernel(plan, *refs), out_shape=(jax.Sh...  37 us

profile of v1, /device:TPU:0, one launch (start us, length us, event | category | flops | bytes accessed | tf_op | source)
XLA Modules:
  0.0 103.7 jit_solution(7422791874192101697)
XLA Ops:
  0.6 37.0 %shard_map.77 = (bf16[8,128,1024]{2,1,0:T(8,128)(2,1)}, f32[2,4,8,128]{3,2,1,0:T(8,128)}) custom-call(bf16[8,64,1024]{2,1,0:T(8,128)(2,1)} %refs_0_.1, s32[8]{0:T(128)} %bitcast.2, bf16[64,1024]{1,0:T(8,128)(2,1)} %refs_2_.1, s32[1,64]{1,0:T(1,128)} %bitcast.3, bf16[8,128,1024]{2,1,0:T(8,128)(2,1)} %refs_4_.1, f32[8]{0:T(128)} %refs_5_.1), custom_call_target="tpu_custom_call" | custom-call | tf_op jit(solution)/shard_map/pallas_call | solution.py:488
  37.7 66.0 %shard_map.78 = (bf16[8,128,1024]{2,1,0:T(8,128)(2,1)}, f32[8,32]{1,0:T(8,128)}) custom-call(bf16[8,128,1024]{2,1,0:T(8,128)(2,1)} %get-tuple-element.4.refs_0_, f32[2,4,8,128]{3,2,1,0:T(8,128)} %get-tuple-element.5.refs_1_), custom_call_target="tpu_custom_call" | custom-call | tf_op jit(solution)/shard_map/pallas_call | solution.py:528

commit v2 on v1

--- a/solution.py
+++ b/solution.py
@@ -179,7 +179,7 @@
     plan,
     stay_ref, count_in, moving_ref, list_in, centre_ref, sharp_in,
     out_ref, mass_ref,
-    count_ref, moving_own, list_ref, sharp_ref, operand_sem, total_buf, mass_col,
+    count_ref, moving_own, list_ref, sharp_ref, operand_sem, total_buf, mass_col, norm_buf,
     stay_buf, count_buf, moving_buf, pos_own, pos_buf, placed, arrived, centre_buf, result_buf, mass_buf,
     stay_send, stay_recv, count_send, count_recv, moving_send, moving_recv, pos_send, pos_recv,
     slot_send, slot_recv, centre_sem, result_send, result_recv, mass_send, mass_recv, local_sem,
@@ -227,6 +227,47 @@
 
     for j in range(half):
         own_copy(j).start()
+
+    pl.semaphore_wait(barrier, len(peers) + len(plane))
+
+    def moving_copy(k):
+        return pltpu.make_async_remote_copy(
+            src_ref=moving_ref, dst_ref=moving_buf.at[k - 1],
+            send_sem=moving_send.at[k - 1], recv_sem=moving_recv.at[k - 1],
+            device_id=(owner, rep_at(k, 0)), device_id_type=MESH,
+        )
+
+    def pos_copy(k):
+        return pltpu.make_async_remote_copy(
+            src_ref=pos_own, dst_ref=pos_buf.at[k - 1],
+            send_sem=pos_send.at[k - 1], recv_sem=pos_recv.at[k - 1],
+            device_id=(owner, rep_at(k, 0)), device_id_type=MESH,
+        )
+
+    for k in range(1, groups):
+        moving_copy(k).start()
+
+    def count_copy(k, dc):
+        q = k * split + dc
+        return pltpu.make_async_remote_copy(
+            src_ref=count_buf.at[0], dst_ref=count_buf.at[q],
+            send_sem=count_send.at[q], recv_sem=count_recv.at[q],
+            device_id=(owner, rep_at(k, dc)), device_id_type=MESH,
+        )
+
+    def stay_copy(j, k, dc):
+        q = k * split + dc
+        return pltpu.make_async_remote_copy(
+            src_ref=stay_ref.at[lax.rem(core + dc, split) * half + j], dst_ref=stay_buf.at[j, q],
+            send_sem=stay_send.at[j, q], recv_sem=stay_recv.at[j, q],
+            device_id=(owner, rep_at(k, dc)), device_id_type=MESH,
+        )
+
+    siblings = [(k, dc) for k, dc in peers if k == 0]
+    distant = [(k, dc) for k, dc in peers if k > 0]
+    for j in range(half):
+        for k, dc in siblings:
+            stay_copy(j, k, dc).start()
 
     moving = plan.moving
     small[0].wait()
@@ -248,50 +289,10 @@
     )
     pos_own[...] = jnp.full(pos_own.shape, -1, jnp.int32)
     pos_own[:, :moving] = jnp.broadcast_to(position, (8, moving))
-
-    pl.semaphore_wait(barrier, len(peers) + len(plane))
-
-    def moving_copy(k):
-        return pltpu.make_async_remote_copy(
-            src_ref=moving_ref, dst_ref=moving_buf.at[k - 1],
-            send_sem=moving_send.at[k - 1], recv_sem=moving_recv.at[k - 1],
-            device_id=(owner, rep_at(k, 0)), device_id_type=MESH,
-        )
-
-    def pos_copy(k):
-        return pltpu.make_async_remote_copy(
-            src_ref=pos_own, dst_ref=pos_buf.at[k - 1],
-            send_sem=pos_send.at[k - 1], recv_sem=pos_recv.at[k - 1],
-            device_id=(owner, rep_at(k, 0)), device_id_type=MESH,
-        )
-
     for k in range(1, groups):
         pos_copy(k).start()
-        moving_copy(k).start()
-
-    def count_copy(k, dc):
-        q = k * split + dc
-        return pltpu.make_async_remote_copy(
-            src_ref=count_buf.at[0], dst_ref=count_buf.at[q],
-            send_sem=count_send.at[q], recv_sem=count_recv.at[q],
-            device_id=(owner, rep_at(k, dc)), device_id_type=MESH,
-        )
-
-    def stay_copy(j, k, dc):
-        q = k * split + dc
-        return pltpu.make_async_remote_copy(
-            src_ref=stay_ref.at[lax.rem(core + dc, split) * half + j], dst_ref=stay_buf.at[j, q],
-            send_sem=stay_send.at[j, q], recv_sem=stay_recv.at[j, q],
-            device_id=(owner, rep_at(k, dc)), device_id_type=MESH,
-        )
-
     for k, dc in peers:
         count_copy(k, dc).start()
-    siblings = [(k, dc) for k, dc in peers if k == 0]
-    distant = [(k, dc) for k, dc in peers if k > 0]
-    for j in range(half):
-        for k, dc in siblings:
-            stay_copy(j, k, dc).start()
     small[2].wait()
     small[3].wait()
 
@@ -333,6 +334,11 @@
         slot_copy(k, dc).start()
     arrived[0] = placed[owner * split + core]
     centre_copy.wait()
+    for j in range(half):
+        wide = centre_buf[j].astype(jnp.float32)
+        norm_buf[j] = jnp.broadcast_to(
+            jnp.sum(wide * wide, axis=1, keepdims=True), norm_buf.shape[1:]
+        )
     for k, dc in peers:
         count_copy(k, dc).wait_recv()
 
@@ -351,14 +357,10 @@
             result_buf.at[j], out_ref.at[core * half + j], result_recv.at[j, 0]
         )
 
-    def list_facts(j):
-        centres = centre_buf[j]
-        wide = centres.astype(jnp.float32)
-        norm = jnp.sum(wide * wide, axis=1, keepdims=True)
-        return centres, norm, sharp_ref[core * half + j]
-
     def add_part(j, rows, mask):
-        num, mass, mass_row = weigh_rows(plan, *list_facts(j), rows, mask)
+        num, mass, mass_row = weigh_rows(
+            plan, centre_buf[j], norm_buf[j][:, 0:1], sharp_ref[core * half + j], rows, mask
+        )
         total_buf[j] += num
         mass_col[j] += jnp.broadcast_to(mass, mass_col.shape[1:])
         mass_buf[j] += mass_row
@@ -375,14 +377,39 @@
         members = stay_buf[j, first:last].reshape((last - first) * capacity, features)
         add_part(j, members, mask)
 
-    def add_arrivals(j):
+    def add_arrivals():
+        fine = plan.fine
+        rows = arrived[:, :, :features].reshape(total, features)
+        marks = arrived[:, :, features:].reshape(total, LANES)
         spread = jnp.full((8, LANES), 1.0 / LANES, jnp.bfloat16)
-        marks = arrived[:, :, features:].reshape(total, LANES)
         present = lax.dot_general(
             spread, marks, (((1,), (1,)), ((), ())), preferred_element_type=jnp.float32
         )[0:1]
-        here = jnp.where(arrived_list == j, present, 0.0)
-        add_part(j, arrived[:, :, :features].reshape(total, features), here)
+        products = lax.dot_general(
+            centre_buf[...].reshape(half * fine, features), rows, (((1,), (1,)), ((), ())),
+            preferred_element_type=jnp.float32,
+        )
+        parts = []
+        for j in range(half):
+            own = products[j * fine : (j + 1) * fine]
+            sharp = sharp_ref[core * half + j]
+            scores = sharp * (2.0 * own - norm_buf[j][:, 0:1]) / math.sqrt(features)
+            raised = jnp.exp(scores - jnp.max(scores, axis=0, keepdims=True))
+            weights = (raised / jnp.sum(raised, axis=0, keepdims=True)).astype(jnp.bfloat16)
+            here = jnp.where(arrived_list == j, present, 0.0)
+            weights = weights * here.astype(jnp.bfloat16)
+            mass = jnp.sum(weights.astype(jnp.float32), axis=1, keepdims=True)
+            mass_col[j] += jnp.broadcast_to(mass, mass_col.shape[1:])
+            parts.append(weights)
+        stacked = jnp.concatenate(parts, axis=0)
+        ones = jnp.ones((8, total), jnp.bfloat16)
+        mass_row = lax.dot_general(
+            ones, stacked, (((1,), (1,)), ((), ())), preferred_element_type=jnp.float32
+        )
+        numerator = jnp.dot(stacked, rows, preferred_element_type=jnp.float32)
+        for j in range(half):
+            mass_buf[j] += mass_row[:, j * fine : (j + 1) * fine]
+            total_buf[j] += numerator[j * fine : (j + 1) * fine]
 
     def add_near(j):
         total_buf[j] = prior_weight * centre_buf[j].astype(jnp.float32)
@@ -418,7 +445,6 @@
         return carry
 
     def settle(j, carry):
-        add_arrivals(j)
         finish(j)
         return carry
 
@@ -427,8 +453,8 @@
     add_near(last)
     for k, dc in sent:
         slot_copy(k, dc).wait_recv()
+    add_arrivals()
     lax.fori_loop(0, last, settle, 0)
-    add_arrivals(last)
     add_far(last)
     finish(last)
 
@@ -462,12 +488,15 @@
         mass_copy(dc).wait()
 
 
-def deliver_kernel(plan, made_ref, mass_ref, out_ref, share_ref, sems):
+def deliver_kernel(plan, made_ref, mass_ref, out_ref, share_ref, held, in_sems, out_sems):
+    fetches = [
+        pltpu.make_async_copy(made_ref.at[i], held.at[i], in_sems.at[i]) for i in range(plan.lists)
+    ]
     copies = [
-        pltpu.make_async_copy(made_ref.at[i], out_ref.at[i], sems.at[i]) for i in range(plan.lists)
+        pltpu.make_async_copy(held.at[i], out_ref.at[i], out_sems.at[i]) for i in range(plan.lists)
     ]
-    for copy in copies:
-        copy.start()
+    for fetch in fetches:
+        fetch.start()
     replica = lax.axis_index("rep")
     width = plan.fine // plan.replicas
     rows = [mass_ref[s, j, 0:1, :] for s in range(plan.split) for j in range(plan.half)]
@@ -476,6 +505,9 @@
     for r in range(1, plan.replicas):
         share = jnp.where(replica == r, whole[:, r * width : (r + 1) * width], share)
     share_ref[...] = share
+    for fetch, copy in zip(fetches, copies):
+        fetch.wait()
+        copy.start()
     for copy in copies:
         copy.wait()
 
@@ -500,6 +532,7 @@
             pltpu.SMEM((plan.lists,), jnp.float32),
             dma((4,)),
             pltpu.VMEM((half, plan.fine, plan.features), jnp.float32),
+            pltpu.VMEM((half, plan.fine, LANES), jnp.float32),
             pltpu.VMEM((half, plan.fine, LANES), jnp.float32),
             pltpu.VMEM((half, replicas, plan.capacity, plan.features), jnp.bfloat16),
             pltpu.VMEM((replicas, plan.lists, members), jnp.int32),
@@ -533,7 +566,9 @@
         ),
         in_specs=[any_space, pl.BlockSpec(memory_space=pltpu.VMEM)],
         out_specs=(any_space, pl.BlockSpec(memory_space=pltpu.VMEM)),
-        scratch_shapes=[dma((plan.lists,))],
+        scratch_shapes=[
+            pltpu.VMEM(centroids.shape, jnp.bfloat16), dma((plan.lists,)), dma((plan.lists,))
+        ],
         compiler_params=pltpu.CompilerParams(vmem_limit_bytes=VMEM_GRANT),
     )(refreshed, mass)
 

time: 104 us -> 41.6 us (0.40)
  Pallas kernels: 103 us -> 40.8 us
    pallas_call x1, Pallas kernels: 66 us -> 3.75 us  [fused(): pl.pallas_call(lambda *refs: deliver_kernel(plan, *refs), out_shape=(jax....]
where the time goes in v2:
time: 41.6 us; the launch traced here: 41.4 us
  Pallas kernels  40.8 us (98%)
  between operations  0.64 us (2%)
    pallas_call x1, Pallas kernels, fused(): pl.pallas_call(lambda *refs: fused_kernel(plan, *refs), out_shape=(jax.Sh...  37 us
    pallas_call x1, Pallas kernels, fused(): pl.pallas_call(lambda *refs: deliver_kernel(plan, *refs), out_shape=(jax....  3.75 us

profile of v2, /device:TPU:0, one launch (start us, length us, event | category | flops | bytes accessed | tf_op | source)
XLA Modules:
  0.0 41.4 jit_solution(7167534522854654129)
XLA Ops:
  0.6 37.0 %shard_map.77 = (bf16[8,128,1024]{2,1,0:T(8,128)(2,1)}, f32[2,4,8,128]{3,2,1,0:T(8,128)}) custom-call(bf16[8,64,1024]{2,1,0:T(8,128)(2,1)} %refs_0_.1, s32[8]{0:T(128)} %bitcast.2, bf16[64,1024]{1,0:T(8,128)(2,1)} %refs_2_.1, s32[1,64]{1,0:T(1,128)} %bitcast.3, bf16[8,128,1024]{2,1,0:T(8,128)(2,1)} %refs_4_.1, f32[8]{0:T(128)} %refs_5_.1), custom_call_target="tpu_custom_call" | custom-call | tf_op jit(solution)/shard_map/pallas_call | solution.py:520
  37.7 3.7 %shard_map.78 = (bf16[8,128,1024]{2,1,0:T(8,128)(2,1)}, f32[8,32]{1,0:T(8,128)}) custom-call(bf16[8,128,1024]{2,1,0:T(8,128)(2,1)} %get-tuple-element.4.refs_0_, f32[2,4,8,128]{3,2,1,0:T(8,128)} %get-tuple-element.5.refs_1_), custom_call_target="tpu_custom_call" | custom-call | tf_op jit(solution)/shard_map/pallas_call | solution.py:561

commit v3 on v2

--- a/solution.py
+++ b/solution.py
@@ -124,7 +124,7 @@
 
 LANES = 128
 VMEM_BUDGET = 40 * 2**20
-VMEM_GRANT = 60000 * 2**10
+VMEM_GRANT = 48 * 2**20
 MESH = pl.DeviceIdType.MESH
 
 
@@ -265,6 +265,10 @@
 
     siblings = [(k, dc) for k, dc in peers if k == 0]
     distant = [(k, dc) for k, dc in peers if k > 0]
+    ahead = min(len(distant) + 1, half * len(distant))
+    for i in range(ahead):
+        j, place = divmod(i, len(distant))
+        stay_copy(j, *distant[place]).start()
     for j in range(half):
         for k, dc in siblings:
             stay_copy(j, k, dc).start()
@@ -309,8 +313,6 @@
     for k in range(1, groups):
         pos_copy(k).wait_send()
         moving_copy(k).wait_send()
-    for k, dc in distant:
-        stay_copy(0, k, dc).start()
     for k in range(1, groups):
         pos_copy(k).wait_recv()
         moving_copy(k).wait_recv()
@@ -421,9 +423,13 @@
         add_stay(j, 0, split)
 
     def pass_on(j):
-        for k, dc in distant:
+        for i, (k, dc) in enumerate(distant):
             stay_copy(j, k, dc).wait_send()
-            stay_copy(j + 1, k, dc).start()
+            step, place = divmod(i + ahead, len(distant))
+
+            @pl.when(j + step < half)
+            def _():
+                stay_copy(j + step, *distant[place]).start()
 
     def add_far(j):
         for k, dc in distant:
@@ -488,30 +494,6 @@
         mass_copy(dc).wait()
 
 
-def deliver_kernel(plan, made_ref, mass_ref, out_ref, share_ref, held, in_sems, out_sems):
-    fetches = [
-        pltpu.make_async_copy(made_ref.at[i], held.at[i], in_sems.at[i]) for i in range(plan.lists)
-    ]
-    copies = [
-        pltpu.make_async_copy(held.at[i], out_ref.at[i], out_sems.at[i]) for i in range(plan.lists)
-    ]
-    for fetch in fetches:
-        fetch.start()
-    replica = lax.axis_index("rep")
-    width = plan.fine // plan.replicas
-    rows = [mass_ref[s, j, 0:1, :] for s in range(plan.split) for j in range(plan.half)]
-    whole = jnp.concatenate(rows, axis=0)
-    share = whole[:, :width]
-    for r in range(1, plan.replicas):
-        share = jnp.where(replica == r, whole[:, r * width : (r + 1) * width], share)
-    share_ref[...] = share
-    for fetch, copy in zip(fetches, copies):
-        fetch.wait()
-        copy.start()
-    for copy in copies:
-        copy.wait()
-
-
 def fused(plan, stay_rows, stay_count, moving_rows, new_list, centroids, sharpness):
     half, split, replicas = plan.half, plan.split, plan.replicas
     any_space = pl.BlockSpec(memory_space=pl.ANY)
@@ -520,8 +502,8 @@
     refreshed, mass = pl.pallas_call(
         lambda *refs: fused_kernel(plan, *refs),
         out_shape=(
-            jax.ShapeDtypeStruct(centroids.shape, jnp.bfloat16),
-            jax.ShapeDtypeStruct((split, half, 8, plan.fine), jnp.float32),
+            pltpu.VMEM(centroids.shape, jnp.bfloat16),
+            pltpu.VMEM((split, half, 8, plan.fine), jnp.float32),
         ),
         in_specs=[pl.BlockSpec(memory_space=pltpu.HBM)] * 6,
         out_specs=(any_space, any_space),
@@ -557,20 +539,17 @@
         compiler_params=pltpu.CompilerParams(
             collective_id=0, has_side_effects=True, vmem_limit_bytes=VMEM_GRANT
         ),
-    )(stay_rows, stay_count.reshape(-1), moving_rows, new_list.reshape(1, -1), centroids, sharpness)
-    return pl.pallas_call(
-        lambda *refs: deliver_kernel(plan, *refs),
-        out_shape=(
-            jax.ShapeDtypeStruct(centroids.shape, jnp.bfloat16),
-            jax.ShapeDtypeStruct((plan.lists, plan.fine // replicas), jnp.float32),
-        ),
-        in_specs=[any_space, pl.BlockSpec(memory_space=pltpu.VMEM)],
-        out_specs=(any_space, pl.BlockSpec(memory_space=pltpu.VMEM)),
-        scratch_shapes=[
-            pltpu.VMEM(centroids.shape, jnp.bfloat16), dma((plan.lists,)), dma((plan.lists,))
-        ],
-        compiler_params=pltpu.CompilerParams(vmem_limit_bytes=VMEM_GRANT),
-    )(refreshed, mass)
+    )(*[
+        pltpu.with_memory_space_constraint(x, pltpu.HBM)
+        for x in (
+            stay_rows, stay_count.reshape(-1), moving_rows, new_list.reshape(1, -1), centroids,
+            sharpness,
+        )
+    ])
+    fine_share = plan.fine // replicas
+    whole = mass[:, :, 0, :].reshape(plan.lists, plan.fine)
+    share = lax.dynamic_slice_in_dim(whole, lax.axis_index("rep") * fine_share, fine_share, 1)
+    return refreshed, share
 
 
 def device_program(stay_rows, stay_count, moving_rows, new_list, centroids, sharpness):

time: 41.6 us -> 41.9 us (level)
  local copies, waits for them, and re-layouts: 0 us -> 1.99 us
  Pallas kernels: 40.8 us -> 39.1 us
    pallas_call x2 -> x1, Pallas kernels: 40.8 us -> 39.1 us  [fused(): pl.pallas_call(lambda *refs: fused_kernel(plan, *refs), out_shape=(pltpu....]
    unnamed x0 -> x1, local copies, waits for them, and re-layouts: none -> 1.32 us
    dynamic_slice x0 -> x1, local copies, waits for them, and re-layouts: none -> 0.67 us  [fused(): lax.dynamic_slice_in_dim(whole, lax.axis_index('rep') * fine_share, fine_...]
where the time goes in v3:
time: 41.9 us; the launch traced here: 41.8 us
  Pallas kernels  39.1 us (93%)
  local copies, waits for them, and re-layouts  1.99 us (5%)
  between operations  0.65 us (2%)
    pallas_call x1, Pallas kernels, fused(): pl.pallas_call(lambda *refs: fused_kernel(plan, *refs), out_shape=(pltpu....  39.1 us
    unnamed x1, local copies, waits for them, and re-layouts  1.32 us

profile of v3, /device:TPU:0, one launch (start us, length us, event | category | flops | bytes accessed | tf_op | source)
XLA Modules:
  0.0 41.8 jit_solution(13269827990260295722)
XLA Ops:
  0.6 39.1 %shard_map.77 = (bf16[8,128,1024]{2,1,0:T(8,128)(2,1)S(1)}, f32[2,4,8,128]{3,2,1,0:T(8,128)S(1)}) custom-call(bf16[8,64,1024]{2,1,0:T(8,128)(2,1)} %refs_0_.1, s32[8]{0:T(128)} %bitcast.4, bf16[64,1024]{1,0:T(8,128)(2,1)} %refs_2_.1, s32[1,64]{1,0:T(1,128)} %bitcast.5, bf16[8,128,1024]{2,1,0:T(8,128)(2,1)} %refs_4_.1, f32[8]{0:T(128)} %refs_5_.1), custom_call_target="tpu_custom_call" | custom-call | tf_op jit(solution)/shard_map/pallas_call | solution.py:502
  39.8 0.7 %constant_dynamic-slice_fusion = f32[8,32]{1,0:T(8,128)} fusion(f32[8,128]{1,0:T(8,128)S(1)} %bitcast.3, s32[]{:T(128)S(6)} %select_n.3), kind=kLoop, calls=%fused_computation | loop fusion | bytes 2052 | tf_op jit(solution)/shard_map/dynamic_slice | solution.py:551
  40.5 1.3 %copy.9 = bf16[8,128,1024]{2,1,0:T(8,128)(2,1)} copy(bf16[8,128,1024]{2,1,0:T(8,128)(2,1)S(1)} %get-tuple-element.6) | data formatting | bytes 4194304
  (1 shorter events, 0.0 us)

commit v4 on v3

--- a/solution.py
+++ b/solution.py
@@ -149,7 +149,7 @@
         small = 2 * (slots + held + centres + gathered)
         return (
             small <= VMEM_BUDGET
-            and self.block % 16 == 0
+            and self.per_source % 8 == 0
             and self.capacity % 16 == 0
             and self.moving % 16 == 0
             and self.features % LANES == 0
@@ -265,10 +265,6 @@
 
     siblings = [(k, dc) for k, dc in peers if k == 0]
     distant = [(k, dc) for k, dc in peers if k > 0]
-    ahead = min(len(distant) + 1, half * len(distant))
-    for i in range(ahead):
-        j, place = divmod(i, len(distant))
-        stay_copy(j, *distant[place]).start()
     for j in range(half):
         for k, dc in siblings:
             stay_copy(j, k, dc).start()
@@ -289,7 +285,7 @@
     slot = jnp.sum(earlier, axis=0, keepdims=True)
     target = list_ref[...]
     position = (
-        (target // half) * plan.block + group * plan.per_source + (target % half) * SLOT_L + slot
+        (target // half) * plan.per_source + (target % half) * SLOT_L + slot
     )
     pos_own[...] = jnp.full(pos_own.shape, -1, jnp.int32)
     pos_own[:, :moving] = jnp.broadcast_to(position, (8, moving))
@@ -300,41 +296,44 @@
     small[2].wait()
     small[3].wait()
 
-    total = plan.blocks * plan.block
-    slot_row = lax.broadcasted_iota(jnp.int32, (total, moving), 0)
-
-    def one_hot(positions):
-        return jnp.where(slot_row == positions, 1.0, 0.0).astype(jnp.bfloat16)
-
-    pick = one_hot(pos_own[0:1, :moving])
+    sent = [(k, dc) for k in range(owners) for dc in range(split) if (k, dc) != (0, 0)]
+    slots = plan.blocks * plan.per_source
+    slot_row = lax.broadcasted_iota(jnp.int32, (slots, moving), 0)
     ones = jnp.ones((moving, LANES), jnp.bfloat16)
-    rows = jnp.dot(pick, moving_own[...], preferred_element_type=jnp.float32)
-    flags = jnp.dot(pick, ones, preferred_element_type=jnp.float32)
+
+    def slot_copy(g, k, dc):
+        b = k * split + dc
+        return pltpu.make_async_remote_copy(
+            src_ref=placed.at[g, owner_at(k) * split + lax.rem(core + dc, split)],
+            dst_ref=arrived.at[g, b],
+            send_sem=slot_send.at[g, b], recv_sem=slot_recv.at[g, b],
+            device_id=(owner_at(k), rep_at(0, dc)), device_id_type=MESH,
+        )
+
+    def place_group(g, positions, source):
+        pick = jnp.where(slot_row == positions, 1.0, 0.0).astype(jnp.bfloat16)
+        rows = jnp.dot(pick, source, preferred_element_type=jnp.float32)
+        flags = jnp.dot(pick, ones, preferred_element_type=jnp.float32)
+        shape = (plan.blocks, plan.per_source)
+        placed[g, :, :, :features] = rows.reshape(*shape, features).astype(jnp.bfloat16)
+        placed[g, :, :, features:] = flags.reshape(*shape, LANES).astype(jnp.bfloat16)
+        for k, dc in sent:
+            slot_copy(g, k, dc).start()
+        arrived[g, 0] = placed[g, owner * split + core]
+
+    place_group(0, pos_own[0:1, :moving], moving_own[...])
     for k in range(1, groups):
         pos_copy(k).wait_send()
         moving_copy(k).wait_send()
+    ahead = min(len(distant) + 1, half * len(distant))
+    for i in range(ahead):
+        j, place = divmod(i, len(distant))
+        stay_copy(j, *distant[place]).start()
     for k in range(1, groups):
         pos_copy(k).wait_recv()
         moving_copy(k).wait_recv()
-        pick = one_hot(pos_buf[k - 1, 0:1, :moving])
-        rows += jnp.dot(pick, moving_buf[k - 1], preferred_element_type=jnp.float32)
-        flags += jnp.dot(pick, ones, preferred_element_type=jnp.float32)
-    placed[:, :, :features] = rows.astype(jnp.bfloat16).reshape(plan.blocks, plan.block, features)
-    placed[:, :, features:] = flags.astype(jnp.bfloat16).reshape(plan.blocks, plan.block, LANES)
-
-    def slot_copy(k, dc):
-        b = k * split + dc
-        return pltpu.make_async_remote_copy(
-            src_ref=placed.at[owner_at(k) * split + lax.rem(core + dc, split)],
-            dst_ref=arrived.at[b],
-            send_sem=slot_send.at[b], recv_sem=slot_recv.at[b],
-            device_id=(owner_at(k), rep_at(0, dc)), device_id_type=MESH,
-        )
-
-    sent = [(k, dc) for k in range(owners) for dc in range(split) if (k, dc) != (0, 0)]
-    for k, dc in sent:
-        slot_copy(k, dc).start()
-    arrived[0] = placed[owner * split + core]
+        place_group(k, pos_buf[k - 1, 0:1, :moving], moving_buf[k - 1])
+    total = groups * slots
     centre_copy.wait()
     for j in range(half):
         wide = centre_buf[j].astype(jnp.float32)
@@ -381,8 +380,8 @@
 
     def add_arrivals():
         fine = plan.fine
-        rows = arrived[:, :, :features].reshape(total, features)
-        marks = arrived[:, :, features:].reshape(total, LANES)
+        rows = arrived[:, :, :, :features].reshape(total, features)
+        marks = arrived[:, :, :, features:].reshape(total, LANES)
         spread = jnp.full((8, LANES), 1.0 / LANES, jnp.bfloat16)
         present = lax.dot_general(
             spread, marks, (((1,), (1,)), ((), ())), preferred_element_type=jnp.float32
@@ -457,8 +456,9 @@
     last = half - 1
     lax.fori_loop(0, last, early, 0)
     add_near(last)
-    for k, dc in sent:
-        slot_copy(k, dc).wait_recv()
+    for g in range(groups):
+        for k, dc in sent:
+            slot_copy(g, k, dc).wait_recv()
     add_arrivals()
     lax.fori_loop(0, last, settle, 0)
     add_far(last)
@@ -483,8 +483,9 @@
     for j in range(half):
         for k, dc in siblings:
             stay_copy(j, k, dc).wait_send()
-    for k, dc in sent:
-        slot_copy(k, dc).wait_send()
+    for g in range(groups):
+        for k, dc in sent:
+            slot_copy(g, k, dc).wait_send()
     for j in range(half):
         result_own(j).wait()
         for dc in range(1, split):
@@ -521,8 +522,8 @@
             pltpu.VMEM((max(1, plan.groups - 1), plan.moving, plan.features), jnp.bfloat16),
             pltpu.VMEM((8, plan.moving_lanes), jnp.int32),
             pltpu.VMEM((max(1, plan.groups - 1), 8, plan.moving_lanes), jnp.int32),
-            pltpu.VMEM((plan.blocks, plan.block, plan.width), jnp.bfloat16),
-            pltpu.VMEM((plan.blocks, plan.block, plan.width), jnp.bfloat16),
+            pltpu.VMEM((plan.groups, plan.blocks, plan.per_source, plan.width), jnp.bfloat16),
+            pltpu.VMEM((plan.groups, plan.blocks, plan.per_source, plan.width), jnp.bfloat16),
             pltpu.VMEM((half, plan.fine, plan.features), jnp.bfloat16),
             pltpu.VMEM((half, plan.fine, plan.features), jnp.bfloat16),
             pltpu.VMEM((half, 8, plan.fine), jnp.float32),
@@ -530,7 +531,7 @@
             dma((replicas,)), dma((replicas,)),
             dma((plan.groups,)), dma((plan.groups,)),
             dma((plan.groups,)), dma((plan.groups,)),
-            dma((plan.blocks,)), dma((plan.blocks,)),
+            dma((plan.groups, plan.blocks)), dma((plan.groups, plan.blocks)),
             dma,
             dma((half, split)), dma((half, split)),
             dma((split,)), dma((split,)),

time: 41.9 us -> 40 us (0.955)
  Pallas kernels: 39.1 us -> 37.2 us
    pallas_call x1, Pallas kernels: 39.1 us -> 37.2 us  [fused(): pl.pallas_call(lambda *refs: fused_kernel(plan, *refs), out_shape=(pltpu....]
where the time goes in v4:
time: 40 us; the launch traced here: 39.9 us
  Pallas kernels  37.2 us (93%)
  local copies, waits for them, and re-layouts  1.99 us (5%)
  between operations  0.65 us (2%)
    pallas_call x1, Pallas kernels, fused(): pl.pallas_call(lambda *refs: fused_kernel(plan, *refs), out_shape=(pltpu....  37.2 us
    unnamed x1, local copies, waits for them, and re-layouts  1.32 us

profile of v4, /device:TPU:0, one launch (start us, length us, event | category | flops | bytes accessed | tf_op | source)
XLA Modules:
  0.0 39.9 jit_solution(18101604693302309239)
XLA Ops:
  0.6 37.2 %shard_map.77 = (bf16[8,128,1024]{2,1,0:T(8,128)(2,1)S(1)}, f32[2,4,8,128]{3,2,1,0:T(8,128)S(1)}) custom-call(bf16[8,64,1024]{2,1,0:T(8,128)(2,1)} %refs_0_.1, s32[8]{0:T(128)} %bitcast.4, bf16[64,1024]{1,0:T(8,128)(2,1)} %refs_2_.1, s32[1,64]{1,0:T(1,128)} %bitcast.5, bf16[8,128,1024]{2,1,0:T(8,128)(2,1)} %refs_4_.1, f32[8]{0:T(128)} %refs_5_.1), custom_call_target="tpu_custom_call" | custom-call | tf_op jit(solution)/shard_map/pallas_call | solution.py:503
  37.9 0.7 %constant_dynamic-slice_fusion = f32[8,32]{1,0:T(8,128)} fusion(f32[8,128]{1,0:T(8,128)S(1)} %bitcast.3, s32[]{:T(128)S(6)} %select_n.3), kind=kLoop, calls=%fused_computation | loop fusion | bytes 2052 | tf_op jit(solution)/shard_map/dynamic_slice | solution.py:552
  38.5 1.3 %copy.9 = bf16[8,128,1024]{2,1,0:T(8,128)(2,1)} copy(bf16[8,128,1024]{2,1,0:T(8,128)(2,1)S(1)} %get-tuple-element.6) | data formatting | bytes 4194304
  (1 shorter events, 0.0 us)

commit v5 on v4

--- a/solution.py
+++ b/solution.py
@@ -265,6 +265,9 @@
 
     siblings = [(k, dc) for k, dc in peers if k == 0]
     distant = [(k, dc) for k, dc in peers if k > 0]
+    ahead = min(len(distant) + 1, half * len(distant))
+    if distant:
+        stay_copy(0, *distant[0]).start()
     for j in range(half):
         for k, dc in siblings:
             stay_copy(j, k, dc).start()
@@ -322,11 +325,7 @@
         arrived[g, 0] = placed[g, owner * split + core]
 
     place_group(0, pos_own[0:1, :moving], moving_own[...])
-    for k in range(1, groups):
-        pos_copy(k).wait_send()
-        moving_copy(k).wait_send()
-    ahead = min(len(distant) + 1, half * len(distant))
-    for i in range(ahead):
+    for i in range(1, ahead):
         j, place = divmod(i, len(distant))
         stay_copy(j, *distant[place]).start()
     for k in range(1, groups):
@@ -476,6 +475,9 @@
     for dc in range(1, split):
         mass_copy(dc).start()
 
+    for k in range(1, groups):
+        pos_copy(k).wait_send()
+        moving_copy(k).wait_send()
     for k, dc in peers:
         count_copy(k, dc).wait_send()
     for k, dc in distant:

time: 40 us -> 40 us (level)
  no operation moved by 1% of the time
where the time goes in v5:
time: 40 us; the launch traced here: 39.9 us
  Pallas kernels  37.2 us (93%)
  local copies, waits for them, and re-layouts  1.99 us (5%)
  between operations  0.65 us (2%)
    pallas_call x1, Pallas kernels, fused(): pl.pallas_call(lambda *refs: fused_kernel(plan, *refs), out_shape=(pltpu....  37.2 us
    unnamed x1, local copies, waits for them, and re-layouts  1.32 us

profile of v5, /device:TPU:0, one launch (start us, length us, event | category | flops | bytes accessed | tf_op | source)
XLA Modules:
  0.0 39.9 jit_solution(10519033866805704453)
XLA Ops:
  0.6 37.2 %shard_map.77 = (bf16[8,128,1024]{2,1,0:T(8,128)(2,1)S(1)}, f32[2,4,8,128]{3,2,1,0:T(8,128)S(1)}) custom-call(bf16[8,64,1024]{2,1,0:T(8,128)(2,1)} %refs_0_.1, s32[8]{0:T(128)} %bitcast.4, bf16[64,1024]{1,0:T(8,128)(2,1)} %refs_2_.1, s32[1,64]{1,0:T(1,128)} %bitcast.5, bf16[8,128,1024]{2,1,0:T(8,128)(2,1)} %refs_4_.1, f32[8]{0:T(128)} %refs_5_.1), custom_call_target="tpu_custom_call" | custom-call | tf_op jit(solution)/shard_map/pallas_call | solution.py:505
  37.9 0.7 %constant_dynamic-slice_fusion = f32[8,32]{1,0:T(8,128)} fusion(f32[8,128]{1,0:T(8,128)S(1)} %bitcast.3, s32[]{:T(128)S(6)} %select_n.3), kind=kLoop, calls=%fused_computation | loop fusion | bytes 2052 | tf_op jit(solution)/shard_map/dynamic_slice | solution.py:554
  38.5 1.3 %copy.9 = bf16[8,128,1024]{2,1,0:T(8,128)(2,1)} copy(bf16[8,128,1024]{2,1,0:T(8,128)(2,1)S(1)} %get-tuple-element.6) | data formatting | bytes 4194304
  (1 shorter events, 0.0 us)

commit v6 on v5

--- a/solution.py
+++ b/solution.py
@@ -268,9 +268,6 @@
     ahead = min(len(distant) + 1, half * len(distant))
     if distant:
         stay_copy(0, *distant[0]).start()
-    for j in range(half):
-        for k, dc in siblings:
-            stay_copy(j, k, dc).start()
 
     moving = plan.moving
     small[0].wait()
@@ -332,6 +329,9 @@
         pos_copy(k).wait_recv()
         moving_copy(k).wait_recv()
         place_group(k, pos_buf[k - 1, 0:1, :moving], moving_buf[k - 1])
+    for j in range(half):
+        for k, dc in siblings:
+            stay_copy(j, k, dc).start()
     total = groups * slots
     centre_copy.wait()
     for j in range(half):
@@ -460,7 +460,9 @@
             slot_copy(g, k, dc).wait_recv()
     add_arrivals()
     lax.fori_loop(0, last, settle, 0)
-    add_far(last)
+    for k, dc in distant:
+        stay_copy(last, k, dc).wait_recv()
+        add_stay(last, k * split + dc, k * split + dc + 1)
     finish(last)
 
     def mass_copy(dc):

time: 40 us -> 40 us (level)
  no operation moved by 1% of the time
where the time goes in v6:
time: 40 us; the launch traced here: 39.8 us
  Pallas kernels  37.2 us (93%)
  local copies, waits for them, and re-layouts  1.99 us (5%)
  between operations  0.65 us (2%)
    pallas_call x1, Pallas kernels, fused(): pl.pallas_call(lambda *refs: fused_kernel(plan, *refs), out_shape=(pltpu....  37.2 us
    unnamed x1, local copies, waits for them, and re-layouts  1.32 us

profile of v6, /device:TPU:0, one launch (start us, length us, event | category | flops | bytes accessed | tf_op | source)
XLA Modules:
  0.0 39.8 jit_solution(4706121442369659954)
XLA Ops:
  0.6 37.2 %shard_map.77 = (bf16[8,128,1024]{2,1,0:T(8,128)(2,1)S(1)}, f32[2,4,8,128]{3,2,1,0:T(8,128)S(1)}) custom-call(bf16[8,64,1024]{2,1,0:T(8,128)(2,1)} %refs_0_.1, s32[8]{0:T(128)} %bitcast.4, bf16[64,1024]{1,0:T(8,128)(2,1)} %refs_2_.1, s32[1,64]{1,0:T(1,128)} %bitcast.5, bf16[8,128,1024]{2,1,0:T(8,128)(2,1)} %refs_4_.1, f32[8]{0:T(128)} %refs_5_.1), custom_call_target="tpu_custom_call" | custom-call | tf_op jit(solution)/shard_map/pallas_call | solution.py:507
  37.9 0.7 %constant_dynamic-slice_fusion = f32[8,32]{1,0:T(8,128)} fusion(f32[8,128]{1,0:T(8,128)S(1)} %bitcast.3, s32[]{:T(128)S(6)} %select_n.3), kind=kLoop, calls=%fused_computation | loop fusion | bytes 2052 | tf_op jit(solution)/shard_map/dynamic_slice | solution.py:556
  38.5 1.3 %copy.9 = bf16[8,128,1024]{2,1,0:T(8,128)(2,1)} copy(bf16[8,128,1024]{2,1,0:T(8,128)(2,1)S(1)} %get-tuple-element.6) | data formatting | bytes 4194304
  (1 shorter events, 0.0 us)

commit v7 on v6

--- a/solution.py
+++ b/solution.py
@@ -265,7 +265,7 @@
 
     siblings = [(k, dc) for k, dc in peers if k == 0]
     distant = [(k, dc) for k, dc in peers if k > 0]
-    ahead = min(len(distant) + 1, half * len(distant))
+    ahead = min(2 * len(distant), half * len(distant))
     if distant:
         stay_copy(0, *distant[0]).start()
 

time: 40 us -> 40 us (level)
  no operation moved by 1% of the time
where the time goes in v7:
time: 40 us; the launch traced here: 39.8 us
  Pallas kernels  37.2 us (93%)
  local copies, waits for them, and re-layouts  1.99 us (5%)
  between operations  0.65 us (2%)
    pallas_call x1, Pallas kernels, fused(): pl.pallas_call(lambda *refs: fused_kernel(plan, *refs), out_shape=(pltpu....  37.2 us
    unnamed x1, local copies, waits for them, and re-layouts  1.32 us

profile of v7, /device:TPU:0, one launch (start us, length us, event | category | flops | bytes accessed | tf_op | source)
XLA Modules:
  0.0 39.8 jit_solution(11043560328758304494)
XLA Ops:
  0.6 37.2 %shard_map.77 = (bf16[8,128,1024]{2,1,0:T(8,128)(2,1)S(1)}, f32[2,4,8,128]{3,2,1,0:T(8,128)S(1)}) custom-call(bf16[8,64,1024]{2,1,0:T(8,128)(2,1)} %refs_0_.1, s32[8]{0:T(128)} %bitcast.4, bf16[64,1024]{1,0:T(8,128)(2,1)} %refs_2_.1, s32[1,64]{1,0:T(1,128)} %bitcast.5, bf16[8,128,1024]{2,1,0:T(8,128)(2,1)} %refs_4_.1, f32[8]{0:T(128)} %refs_5_.1), custom_call_target="tpu_custom_call" | custom-call | tf_op jit(solution)/shard_map/pallas_call | solution.py:507
  37.9 0.7 %constant_dynamic-slice_fusion = f32[8,32]{1,0:T(8,128)} fusion(f32[8,128]{1,0:T(8,128)S(1)} %bitcast.3, s32[]{:T(128)S(6)} %select_n.3), kind=kLoop, calls=%fused_computation | loop fusion | bytes 2052 | tf_op jit(solution)/shard_map/dynamic_slice | solution.py:556
  38.5 1.3 %copy.9 = bf16[8,128,1024]{2,1,0:T(8,128)(2,1)} copy(bf16[8,128,1024]{2,1,0:T(8,128)(2,1)S(1)} %get-tuple-element.6) | data formatting | bytes 4194304
  (1 shorter events, 0.0 us)
